TPU v7x, 32 devices: a whole 2x2x4 slice. The times are simulated.
32 devices in a mesh: dp: 8 (over y, x, core), seq: 4 (over z).
Axes of the slice: x: 2, y: 2, z: 4, core: 2. Of those that a mesh axis runs over, the one named last changes fastest.
Arguments:
- inputs: bfloat16 [32, 1024, 1024], P('dp', 'seq'), may hold values from -6 to 6
- doc_ids: int32 [32, 1024], P('dp'), may hold values from 0 to 4, as said below
- cotangent: bfloat16 [32, 1024, 1024], P('dp', 'seq'), may hold values from -6 to 6
- norm_gains: float32 [2, 1024], P(None, ('dp', 'seq')), may hold values from 0.2 to 2
- gains_first: float32 [2, 1024], P(None, ('dp', 'seq')), may hold values from -0.0008544922 to 0.0008544922
- gains_second: float32 [2, 1024], P(None, ('dp', 'seq')), may hold values from 1.6348702e-08 to 6.403242e-08
- kernel: float32 [3, 1024], P(None, ('dp', 'seq')), may hold values from -3.5 to 3.5
- kernel_first: float32 [3, 1024], P(None, ('dp', 'seq')), may hold values from -0.00061035156 to 0.00061035156
- kernel_second: float32 [3, 1024], P(None, ('dp', 'seq')), may hold values from 7.220677e-09 to 2.8610229e-08
- w_in: float32 [1024, 3072], P(('dp', 'seq')), may hold values from -0.1875 to 0.1875
- w_in_first: float32 [1024, 3072], P(('dp', 'seq')), may hold values from -0.00061035156 to 0.00061035156
- w_in_second: float32 [1024, 3072], P(('dp', 'seq')), may hold values from 7.220677e-09 to 2.8610229e-08
- w_out: float32 [1024, 1024], P(('dp', 'seq')), may hold values from -0.1875 to 0.1875
- w_out_first: float32 [1024, 1024], P(('dp', 'seq')), may hold values from -0.00061035156 to 0.00061035156
- w_out_second: float32 [1024, 1024], P(('dp', 'seq')), may hold values from 7.220677e-09 to 2.8610229e-08
- w_gate: float32 [1024, 4608], P(('dp', 'seq')), may hold values from -0.1875 to 0.1875
- w_gate_first: float32 [1024, 4608], P(('dp', 'seq')), may hold values from -0.00030517578 to 0.00030517578
- w_gate_second: float32 [1024, 4608], P(('dp', 'seq')), may hold values from 1.7711095e-09 to 7.220677e-09
- w_up: float32 [1024, 4608], P(('dp', 'seq')), may hold values from -0.1875 to 0.1875
- w_up_first: float32 [1024, 4608], P(('dp', 'seq')), may hold values from -0.00030517578 to 0.00030517578
- w_up_second: float32 [1024, 4608], P(('dp', 'seq')), may hold values from 1.7711095e-09 to 7.220677e-09
- w_down: float32 [4608, 1024], P(('dp', 'seq')), may hold values from -0.09375 to 0.09375
- w_down_first: float32 [4608, 1024], P(('dp', 'seq')), may hold values from -0.00030517578 to 0.00030517578
- w_down_second: float32 [4608, 1024], P(('dp', 'seq')), may hold values from 1.7711095e-09 to 7.220677e-09
Outputs:
- block_out: bfloat16 [32, 1024, 1024], P('dp', 'seq')
- input_grad: float32 [32, 1024, 1024], P('dp', 'seq')
- grad_norm: float32 [], replicated
- gains_first_new: float32 [2, 1024], P(None, ('dp', 'seq'))
- gains_second_new: float32 [2, 1024], P(None, ('dp', 'seq'))
- gains_new: float32 [2, 1024], P(None, ('dp', 'seq'))
- kernel_first_new: float32 [3, 1024], P(None, ('dp', 'seq'))
- updated_tap_variance: float32 [3, 1024], P(None, ('dp', 'seq'))
- kernel_new: float32 [3, 1024], P(None, ('dp', 'seq'))
- w_in_first_new: float32 [1024, 3072], P(('dp', 'seq'))
- w_in_second_new: float32 [1024, 3072], P(('dp', 'seq'))
- w_in_new: float32 [1024, 3072], P(('dp', 'seq'))
- w_out_first_new: float32 [1024, 1024], P(('dp', 'seq'))
- w_out_second_new: float32 [1024, 1024], P(('dp', 'seq'))
- w_out_new: float32 [1024, 1024], P(('dp', 'seq'))
- w_gate_first_new: float32 [1024, 4608], P(('dp', 'seq'))
- w_gate_second_new: float32 [1024, 4608], P(('dp', 'seq'))
- w_gate_new: float32 [1024, 4608], P(('dp', 'seq'))
- w_up_first_new: float32 [1024, 4608], P(('dp', 'seq'))
- w_up_second_new: float32 [1024, 4608], P(('dp', 'seq'))
- w_up_new: float32 [1024, 4608], P(('dp', 'seq'))
- w_down_first_new: float32 [4608, 1024], P(('dp', 'seq'))
- w_down_second_new: float32 [4608, 1024], P(('dp', 'seq'))
- w_down_new: float32 [4608, 1024], P(('dp', 'seq'))
Inputs may be any that keep to these rules, and one draw needn't show every extreme that they name: `doc_ids`: each sequence holds exactly five documents: numbers start at 0 at its first token and rise by one at each document's first token; tokens with equal numbers belong to one document.
All inputs are finite; a program needn't handle non-finite values.
Results may differ from a plain program's by a relative error of at most 0.012.
The roundings to bfloat16 on the way count: a program that leaves them out, or rounds other values in their place, can miss the bound.
Values may be sent and summed in bfloat16 or wider, within the bound.
A program may use at most 320 MiB of HBM per device.

v0:
```python
import math

import jax
import jax.numpy as jnp
from jax import lax
from jax.sharding import PartitionSpec as P

D = 1024
FF = 4608
STEP = 10


EPS_NORM = 1e-05
BETA_ONE = 0.9
BETA_TWO = 0.95
ADAM_EPS = 1e-08
DECAY = 0.1
RATE = 2.0
CLIP = 1.0


def from_behind(shard, axis, by):
    devices = lax.axis_size(axis)
    pairs = [(i, i + by) for i in range(devices) if 0 <= i + by < devices]
    return lax.ppermute(shard, axis, pairs)


def adam_update(master, first, second, gradient, factor, rate):
    clipped = gradient * factor
    new_first = BETA_ONE * first + (1.0 - BETA_ONE) * clipped
    new_second = BETA_TWO * second + (1.0 - BETA_TWO) * clipped * clipped
    first_hat = new_first / (1.0 - BETA_ONE**STEP)
    second_hat = new_second / (1.0 - BETA_TWO**STEP)
    new_master = master - rate * (first_hat / (jnp.sqrt(second_hat) + ADAM_EPS) + DECAY * master)
    return (new_first, new_second, new_master)


def local(
    inputs,
    doc_ids,
    cotangent,
    norm_gains,
    gains_first,
    gains_second,
    kernel,
    kernel_first,
    kernel_second,
    w_in,
    w_in_first,
    w_in_second,
    w_out,
    w_out_first,
    w_out_second,
    w_gate,
    w_gate_first,
    w_gate_second,
    w_up,
    w_up_first,
    w_up_second,
    w_down,
    w_down_first,
    w_down_second,
):
    low_gains = norm_gains.astype(jnp.bfloat16)
    low_kernel = kernel.astype(jnp.bfloat16)
    low_in = w_in.astype(jnp.bfloat16)
    low_out = w_out.astype(jnp.bfloat16)
    low_gate = w_gate.astype(jnp.bfloat16)
    low_up = w_up.astype(jnp.bfloat16)
    low_down = w_down.astype(jnp.bfloat16)
    gathered = (
        lax.all_gather(low_gains, ("dp", "seq"), axis=1, tiled=True),
        lax.all_gather(low_kernel, ("dp", "seq"), axis=1, tiled=True),
        lax.all_gather(low_in, ("dp", "seq"), axis=0, tiled=True),
        lax.all_gather(low_out, ("dp", "seq"), axis=0, tiled=True),
        lax.all_gather(low_gate, ("dp", "seq"), axis=0, tiled=True),
        lax.all_gather(low_up, ("dp", "seq"), axis=0, tiled=True),
        lax.all_gather(low_down, ("dp", "seq"), axis=0, tiled=True),
    )
    (
        full_gains,
        full_kernel,
        collected_entry_matrix,
        gathered_output_weight,
        gathered_gate_weight,
        gathered_up_weight,
        gathered_down_weight,
    ) = gathered
    gain_wide = full_gains.astype(jnp.float32)
    taps = full_kernel.astype(jnp.float32)
    width = inputs.shape[2]
    span = inputs.shape[1]
    position = lax.axis_index("seq") * span
    padded_ids = jnp.pad(doc_ids, ((0, 0), (2, 2)), constant_values=-1)
    near_ids = lax.dynamic_slice_in_dim(padded_ids, position, span + 4, 1)
    centre = near_ids[:, 2 : span + 2]
    same_one = (near_ids[:, 1 : span + 1] == centre).astype(jnp.float32)[..., None]
    matching_lag_pair = (near_ids[:, :span] == centre).astype(jnp.float32)[..., None]
    next_one = (near_ids[:, 3 : span + 3] == centre).astype(jnp.float32)[..., None]
    next_two = (near_ids[:, 4 : span + 4] == centre).astype(jnp.float32)[..., None]
    values = inputs.astype(jnp.float32)
    scale_one = lax.rsqrt(jnp.mean(values * values, axis=-1, keepdims=True) + EPS_NORM)
    rescaled_source = (values * scale_one * gain_wide[0]).astype(jnp.bfloat16)
    mixed_columns = jnp.einsum(
        "uwt,tf->uwf", rescaled_source, collected_entry_matrix, preferred_element_type=jnp.float32
    )
    part_b = mixed_columns[..., :width]
    part_c = mixed_columns[..., width : 2 * width]
    part_x = mixed_columns[..., 2 * width :]
    gated = (part_b * part_x).astype(jnp.bfloat16)
    upper_rim = from_behind(gated[:, span - 2 :], "seq", 1)
    extended = jnp.concatenate([upper_rim, gated], axis=1).astype(jnp.float32)
    lag_one = extended[:, 1 : span + 1] * same_one
    lag_two = extended[:, :span] * matching_lag_pair
    current = extended[:, 2:]
    conv_out = current * taps[2] + lag_one * taps[1] + lag_two * taps[0]
    branch_values = (part_c * conv_out).astype(jnp.bfloat16)
    hidden_one = values + jnp.einsum(
        "uwt,tf->uwf", branch_values, gathered_output_weight, preferred_element_type=jnp.float32
    )
    scale_two = lax.rsqrt(jnp.mean(hidden_one * hidden_one, axis=-1, keepdims=True) + EPS_NORM)
    second_normed_input = (hidden_one * scale_two * gain_wide[1]).astype(jnp.bfloat16)
    gate_preactivation = jnp.einsum(
        "wyz,zm->wym", second_normed_input, gathered_gate_weight, preferred_element_type=jnp.float32
    )
    up_preactivation = jnp.einsum(
        "wyz,zm->wym", second_normed_input, gathered_up_weight, preferred_element_type=jnp.float32
    )
    sigma = jax.nn.sigmoid(gate_preactivation)
    silu_val = gate_preactivation * sigma
    activated_hidden = (silu_val * up_preactivation).astype(jnp.bfloat16)
    block_out = (
        hidden_one
        + jnp.einsum(
            "vyk,kx->vyx",
            activated_hidden,
            gathered_down_weight,
            preferred_element_type=jnp.float32,
        )
    ).astype(jnp.bfloat16)
    activated_gradient = jnp.einsum(
        "uar,tr->uat", cotangent, gathered_down_weight, preferred_element_type=jnp.float32
    )
    down_weight_gradient = jnp.einsum(
        "vna,vnw->aw", activated_hidden, cotangent, preferred_element_type=jnp.float32
    )
    gate_input_gradient = (
        activated_gradient * up_preactivation * sigma * (1.0 + gate_preactivation * (1.0 - sigma))
    ).astype(jnp.bfloat16)
    up_input_gradient = (activated_gradient * silu_val).astype(jnp.bfloat16)
    second_normed_gradient = jnp.einsum(
        "npg,kg->npk", gate_input_gradient, gathered_gate_weight, preferred_element_type=jnp.float32
    )
    second_normed_gradient = second_normed_gradient + jnp.einsum(
        "npg,kg->npk", up_input_gradient, gathered_up_weight, preferred_element_type=jnp.float32
    )
    gate_weight_gradient = jnp.einsum(
        "rbz,rbx->zx", second_normed_input, gate_input_gradient, preferred_element_type=jnp.float32
    )
    up_weight_gradient = jnp.einsum(
        "rbz,rbx->zx", second_normed_input, up_input_gradient, preferred_element_type=jnp.float32
    )
    gain_two_grad = jnp.sum(second_normed_gradient * hidden_one * scale_two, axis=(0, 1))
    zeta_two = second_normed_gradient * gain_wide[1]
    d_hidden = (
        cotangent.astype(jnp.float32)
        + scale_two * zeta_two
        - hidden_one * scale_two**3 * jnp.mean(zeta_two * hidden_one, axis=-1, keepdims=True)
    )
    branch_output_gradient = d_hidden.astype(jnp.bfloat16)
    branch_gradient = jnp.einsum(
        "fxh,dh->fxd",
        branch_output_gradient,
        gathered_output_weight,
        preferred_element_type=jnp.float32,
    )
    output_weight_gradient = jnp.einsum(
        "ncr,ncj->rj", branch_values, branch_output_gradient, preferred_element_type=jnp.float32
    )
    d_part_c = branch_gradient * conv_out
    d_conv = (branch_gradient * part_c).astype(jnp.bfloat16)
    lower_rim = from_behind(d_conv[:, :2], "seq", -1)
    conv_ext = jnp.concatenate([d_conv, lower_rim], axis=1).astype(jnp.float32)
    d_conv_own = conv_ext[:, :span]
    d_gated = (
        d_conv_own * taps[2]
        + conv_ext[:, 1 : span + 1] * next_one * taps[1]
        + conv_ext[:, 2:] * next_two * taps[0]
    )
    kernel_grad = jnp.stack(
        [
            jnp.sum(d_conv_own * lag_two, axis=(0, 1)),
            jnp.sum(d_conv_own * lag_one, axis=(0, 1)),
            jnp.sum(d_conv_own * current, axis=(0, 1)),
        ]
    )
    convolved_derivative = jnp.concatenate(
        [d_gated * part_x, d_part_c, d_gated * part_b], axis=-1
    ).astype(jnp.bfloat16)
    normed_gradient = jnp.einsum(
        "fxh,dh->fxd",
        convolved_derivative,
        collected_entry_matrix,
        preferred_element_type=jnp.float32,
    )
    input_weight_gradient = jnp.einsum(
        "ncr,ncj->rj", rescaled_source, convolved_derivative, preferred_element_type=jnp.float32
    )
    first_scale_derivative = jnp.sum(normed_gradient * values * scale_one, axis=(0, 1))
    zeta_one = normed_gradient * gain_wide[0]
    input_grad = (
        d_hidden
        + scale_one * zeta_one
        - values * scale_one**3 * jnp.mean(zeta_one * values, axis=-1, keepdims=True)
    )
    gains_grad = jnp.stack([first_scale_derivative, gain_two_grad])
    shards = (
        lax.psum_scatter(gains_grad, ("dp", "seq"), scatter_dimension=1, tiled=True),
        lax.psum_scatter(kernel_grad, ("dp", "seq"), scatter_dimension=1, tiled=True),
        lax.psum_scatter(input_weight_gradient, ("dp", "seq"), scatter_dimension=0, tiled=True),
        lax.psum_scatter(output_weight_gradient, ("dp", "seq"), scatter_dimension=0, tiled=True),
        lax.psum_scatter(gate_weight_gradient, ("dp", "seq"), scatter_dimension=0, tiled=True),
        lax.psum_scatter(up_weight_gradient, ("dp", "seq"), scatter_dimension=0, tiled=True),
        lax.psum_scatter(down_weight_gradient, ("dp", "seq"), scatter_dimension=0, tiled=True),
    )
    squares = jnp.float32(0.0)
    for portion in shards:
        squares = squares + jnp.sum(portion * portion)
    grad_norm = jnp.sqrt(lax.psum(squares, ("dp", "seq")))
    factor = CLIP / jnp.maximum(grad_norm, CLIP)
    matrix_rate = RATE / math.sqrt(D)
    gains_first_new, gains_second_new, gains_new = adam_update(
        norm_gains, gains_first, gains_second, shards[0], factor, RATE * 0.3
    )
    kernel_first_new, updated_tap_variance, kernel_new = adam_update(
        kernel, kernel_first, kernel_second, shards[1], factor, RATE * 0.6
    )
    w_in_first_new, w_in_second_new, w_in_new = adam_update(
        w_in, w_in_first, w_in_second, shards[2], factor, matrix_rate
    )
    w_out_first_new, w_out_second_new, w_out_new = adam_update(
        w_out, w_out_first, w_out_second, shards[3], factor, matrix_rate
    )
    w_gate_first_new, w_gate_second_new, w_gate_new = adam_update(
        w_gate, w_gate_first, w_gate_second, shards[4], factor, matrix_rate
    )
    w_up_first_new, w_up_second_new, w_up_new = adam_update(
        w_up, w_up_first, w_up_second, shards[5], factor, matrix_rate
    )
    w_down_first_new, w_down_second_new, w_down_new = adam_update(
        w_down, w_down_first, w_down_second, shards[6], factor, RATE / math.sqrt(FF)
    )
    return (
        block_out,
        input_grad,
        grad_norm,
        gains_first_new,
        gains_second_new,
        gains_new,
        kernel_first_new,
        updated_tap_variance,
        kernel_new,
        w_in_first_new,
        w_in_second_new,
        w_in_new,
        w_out_first_new,
        w_out_second_new,
        w_out_new,
        w_gate_first_new,
        w_gate_second_new,
        w_gate_new,
        w_up_first_new,
        w_up_second_new,
        w_up_new,
        w_down_first_new,
        w_down_second_new,
        w_down_new,
    )


def solution(mesh):
    return jax.shard_map(
        local,
        mesh=mesh,
        in_specs=(
            P("dp", "seq", None),
            P("dp", None),
            P("dp", "seq", None),
            P(None, ("dp", "seq")),
            P(None, ("dp", "seq")),
            P(None, ("dp", "seq")),
            P(None, ("dp", "seq")),
            P(None, ("dp", "seq")),
            P(None, ("dp", "seq")),
            P(("dp", "seq"), None),
            P(("dp", "seq"), None),
            P(("dp", "seq"), None),
            P(("dp", "seq"), None),
            P(("dp", "seq"), None),
            P(("dp", "seq"), None),
            P(("dp", "seq"), None),
            P(("dp", "seq"), None),
            P(("dp", "seq"), None),
            P(("dp", "seq"), None),
            P(("dp", "seq"), None),
            P(("dp", "seq"), None),
            P(("dp", "seq"), None),
            P(("dp", "seq"), None),
            P(("dp", "seq"), None),
        ),
        out_specs=(
            P("dp", "seq", None),
            P("dp", "seq", None),
            P(),
            P(None, ("dp", "seq")),
            P(None, ("dp", "seq")),
            P(None, ("dp", "seq")),
            P(None, ("dp", "seq")),
            P(None, ("dp", "seq")),
            P(None, ("dp", "seq")),
            P(("dp", "seq"), None),
            P(("dp", "seq"), None),
            P(("dp", "seq"), None),
            P(("dp", "seq"), None),
            P(("dp", "seq"), None),
            P(("dp", "seq"), None),
            P(("dp", "seq"), None),
            P(("dp", "seq"), None),
            P(("dp", "seq"), None),
            P(("dp", "seq"), None),
            P(("dp", "seq"), None),
            P(("dp", "seq"), None),
            P(("dp", "seq"), None),
            P(("dp", "seq"), None),
            P(("dp", "seq"), None),
        ),
        check_vma=False,
    )
```

profile of v0, /device:TPU:0, one launch (start us, length us, event | category | flops | bytes accessed | tf_op | source)
XLA Modules:
  0.0 1780.9 jit_solution(18327891600781668823)
XLA Ops:
  16.5 69.6 %all-gather = bf16[32,32,2]{1,2,0:T(2,128)(2,1)S(1)} all-gather(bf16[1,32,2]{1,2,0:T(2,128)(2,1)S(1)} %convert_bitcast_fusion.1), channel_id=1, replica_groups=mesh['dp'=8,'seq'=4] {'dp','seq'}, dimensions={0}, use_global_device_ids=true | all-gather | bytes 4224 | tf_op jit(solution)/shard_map/all_gather | solution.py:72
  86.2 63.5 %all-gather.1 = bf16[32,32,3]{1,2,0:T(4,128)(2,1)S(1)} all-gather(bf16[1,32,3]{1,2,0:T(4,128)(2,1)S(1)} %convert_bitcast_fusion), channel_id=1, replica_groups=mesh['dp'=8,'seq'=4] {'dp','seq'}, dimensions={0}, use_global_device_ids=true | all-gather | bytes 6336 | tf_op jit(solution)/shard_map/all_gather | solution.py:73
  180.0 46.5 %all-gather.14.cloned.1.call-done = bf16[1024,4608]{1,0:T(8,128)(2,1)} async-done(((bf16[32,4608]{1,0:T(8,128)(2,1)}), bf16[1024,4608]{1,0:T(8,128)(2,1)}) %all-gather.14.cloned.1.call-update) | async-done | bytes 9437200 | tf_op jit(solution)/shard_map/all_gather | solution.py:77
  226.5 16.0 fusion.7
  242.5 67.9 %all-gather.16.cloned.1.call-done = bf16[4608,1024]{1,0:T(8,128)(2,1)} async-done(((bf16[144,1024]{1,0:T(8,128)(2,1)}), bf16[4608,1024]{1,0:T(8,128)(2,1)}) %all-gather.16.cloned.1.call-update) | async-done | bytes 9437200 | tf_op jit(solution)/shard_map/all_gather | solution.py:78
  310.4 16.9 fusion.1
  327.2 67.0 %all-gather.12.cloned.1.call-done = bf16[1024,4608]{1,0:T(8,128)(2,1)} async-done(((bf16[32,4608]{1,0:T(8,128)(2,1)}), bf16[1024,4608]{1,0:T(8,128)(2,1)}) %all-gather.12.cloned.1.call-update) | async-done | bytes 9437200 | tf_op jit(solution)/shard_map/all_gather | solution.py:76
  394.3 30.7 %multiply_convert_fusion.1 = (bf16[4,256,4608]{2,1,0:T(8,128)(2,1)}, bf16[4,256,4608]{2,1,0:T(8,128)(2,1)}, bf16[4,256,4608]{2,1,0:T(8,128)(2,1)}) fusion(f32[4,256,4608]{2,1,0:T(8,128)} %fusion.1, f32[4,256,4608]{2,1,0:T(8,128)} %fusion.7, bf16[4,256,1024]{2,1,0:T(8,128)(2,1)S(1)} %multiply_convert_fusion.7, ...), kind=kOutput, calls=%fused_computation.1 | convolution fusion | flops 9734455296 | bytes 77594624 | tf_op jit(solution)/shard_map/wyz,zm->wym/dot_general | solution.py:123
  425.0 16.0 fusion.5
  441.0 16.6 multiply_reduce_fusion.3
  484.9 12.3 fusion.24
  507.2 14.2 convolution_bitcast_fusion.3
  521.5 17.0 convolution_bitcast_fusion.2
  538.7 16.9 convolution_bitcast_fusion.1
  555.7 16.8 convolution_bitcast_fusion
  572.5 16.8 add_convert_fusion
  589.4 41.7 %reduce-scatter.22.cloned.1.call-done = f32[32,2]{1,0:T(8,128)} async-done(((f32[1024,2]{1,0:T(8,128)}), f32[32,2]{1,0:T(8,128)}) %reduce-scatter.22.cloned.1.call-update) | async-done | bytes 272
  632.5 131.9 %reduce-scatter.24.cloned.1.call-done = f32[32,3]{1,0:T(8,128)} async-done(((f32[1024,3]{1,0:T(8,128)}), f32[32,3]{1,0:T(8,128)}) %reduce-scatter.24.cloned.1.call-update) | async-done | bytes 400
  767.0 143.5 %reduce-scatter.14.cloned.1.call-done = f32[32,1024]{1,0:T(8,128)} async-done(((f32[1024,1024]{1,0:T(8,128)}), f32[32,1024]{1,0:T(8,128)}) %reduce-scatter.14.cloned.1.call-update) | async-done | bytes 131088 | tf_op jit(solution)/shard_map/reduce_scatter | solution.py:221
  912.1 159.1 %reduce-scatter.12.cloned.1.call-done = f32[32,3072]{1,0:T(8,128)} async-done(((f32[1024,3072]{1,0:T(8,128)}), f32[32,3072]{1,0:T(8,128)}) %reduce-scatter.12.cloned.1.call-update) | async-done | bytes 393232 | tf_op jit(solution)/shard_map/reduce_scatter | solution.py:220
  1074.3 210.3 %reduce-scatter.16.cloned.1.call-done = f32[32,4608]{1,0:T(8,128)} async-done(((f32[1024,4608]{1,0:T(8,128)}), f32[32,4608]{1,0:T(8,128)}) %reduce-scatter.16.cloned.1.call-update) | async-done | bytes 589840 | tf_op jit(solution)/shard_map/reduce_scatter | solution.py:222
  1287.1 210.8 %reduce-scatter.18.cloned.1.call-done = f32[32,4608]{1,0:T(8,128)} async-done(((f32[1024,4608]{1,0:T(8,128)}), f32[32,4608]{1,0:T(8,128)}) %reduce-scatter.18.cloned.1.call-update) | async-done | bytes 589840 | tf_op jit(solution)/shard_map/reduce_scatter | solution.py:223
  1500.4 210.6 %reduce-scatter.20.cloned.1.call-done = f32[144,1024]{1,0:T(8,128)} async-done(((f32[4608,1024]{1,0:T(8,128)}), f32[144,1024]{1,0:T(8,128)}) %reduce-scatter.20.cloned.1.call-update) | async-done | bytes 589840 | tf_op jit(solution)/shard_map/reduce_scatter | solution.py:224
  1719.0 39.1 %psum.7 = f32[]{:T(128)} all-reduce(f32[]{:T(128)S(6)} %add.212), channel_id=1, replica_groups=mesh['dp'=8,'seq'=4] {'dp','seq'}, use_global_device_ids=true, to_apply=%region_23.24 | all-reduce | flops 1 | bytes 8 | tf_op jit(solution)/shard_map/psum | solution.py:229
  (173 shorter events, 107.4 us)
Async XLA Ops:
  7.2 79.0 %copy-start.37 = (f32[3,32]{1,0:T(4,128)S(1)}, f32[3,32]{1,0:T(4,128)}, u32[]{:S(2)}) copy-start(f32[3,32]{1,0:T(4,128)} %param.30) | copy-start | bytes 1156
  7.2 142.7 %copy-start.6 = (bf16[4,256,1024]{2,1,0:T(8,128)(2,1)S(1)}, bf16[4,256,1024]{2,1,0:T(8,128)(2,1)}, u32[]{:S(2)}) copy-start(bf16[4,256,1024]{2,1,0:T(8,128)(2,1)} %param.24) | copy-start | bytes 6291460
  7.2 143.9 %all-gather.8.cloned.1.call-start = ((), (), s32[]{:S(2)}) async-start(), calls=%async_computation.7 | async-start | bytes 6488064 | tf_op jit(solution)/shard_map/all_gather | solution.py:74
  9.1 163.8 %all-gather.10.cloned.1.call-start = ((), (), s32[]{:S(2)}) async-start(), calls=%async_computation.8 | async-start | bytes 2162688 | tf_op jit(solution)/shard_map/all_gather | solution.py:75
  10.8 215.7 %all-gather.14.cloned.1.call-start = ((), (), s32[]{:S(2)}) async-start(), calls=%async_computation.10 | async-start | bytes 9732096 | tf_op jit(solution)/shard_map/all_gather | solution.py:77
  12.6 297.7 %all-gather.16.cloned.1.call-start = ((), (), s32[]{:S(2)}) async-start(), calls=%async_computation.11 | async-start | bytes 9732096 | tf_op jit(solution)/shard_map/all_gather | solution.py:78
  14.5 379.7 %all-gather.12.cloned.1.call-start = ((), (), s32[]{:S(2)}) async-start(), calls=%async_computation.9 | async-start | bytes 9732096 | tf_op jit(solution)/shard_map/all_gather | solution.py:76
  16.4 614.7 %reduce-scatter.22.cloned.1.call-start = ((), (), s32[]{:S(2)}) async-start(), calls=%async_computation.17 | async-start | bytes 540672
  160.9 5.6 collective-permute-start
  180.0 214.3 %copy-start.15 = (bf16[4,256,1024]{2,1,0:T(8,128)(2,1)}, bf16[4,256,1024]{2,1,0:T(8,128)(2,1)S(1)}, u32[]{:S(2)}) copy-start(bf16[4,256,1024]{2,1,0:T(8,128)(2,1)S(1)} %multiply_convert_fusion.7) | copy-start | bytes 6291460
  468.6 5.8 collective-permute-start.1
  498.2 266.1 %reduce-scatter.24.cloned.1.call-start = ((), (), s32[]{:S(2)}) async-start(), calls=%async_computation.18 | async-start | bytes 540672
  499.4 411.2 %reduce-scatter.14.cloned.1.call-start = ((), (), s32[]{:S(2)}) async-start(), calls=%async_computation.13 | async-start | bytes 4325376 | tf_op jit(solution)/shard_map/reduce_scatter | solution.py:221
  506.6 564.6 %reduce-scatter.12.cloned.1.call-start = ((), (), s32[]{:S(2)}) async-start(), calls=%async_computation.12 | async-start | bytes 12976128 | tf_op jit(solution)/shard_map/reduce_scatter | solution.py:220
  521.4 763.2 %reduce-scatter.16.cloned.1.call-start = ((), (), s32[]{:S(2)}) async-start(), calls=%async_computation.14 | async-start | bytes 19464192 | tf_op jit(solution)/shard_map/reduce_scatter | solution.py:222
  538.5 959.4 %reduce-scatter.18.cloned.1.call-start = ((), (), s32[]{:S(2)}) async-start(), calls=%async_computation.15 | async-start | bytes 19464192 | tf_op jit(solution)/shard_map/reduce_scatter | solution.py:223
  555.6 1155.3 %reduce-scatter.20.cloned.1.call-start = ((), (), s32[]{:S(2)}) async-start(), calls=%async_computation.16 | async-start | bytes 19464192 | tf_op jit(solution)/shard_map/reduce_scatter | solution.py:224
  572.5 1140.9 %copy-start.29 = (f32[4,256]{1,0:T(4,128)S(1)}, f32[4,256]{1,0:T(4,128)}, u32[]{:S(2)}) copy-start(f32[4,256]{1,0:T(4,128)} %get-tuple-element.72) | copy-start | bytes 12292
  1713.5 47.9 %copy-start.17 = (f32[32,1024]{1,0:T(8,128)S(1)}, f32[32,1024]{1,0:T(8,128)}, u32[]{:S(2)}) copy-start(f32[32,1024]{1,0:T(8,128)} %param.36) | copy-start | bytes 393220
  1713.5 52.2 %copy-start.8 = (f32[144,1024]{1,0:T(8,128)S(1)}, f32[144,1024]{1,0:T(8,128)}, u32[]{:S(2)}) copy-start(f32[144,1024]{1,0:T(8,128)} %param.45) | copy-start | bytes 1769476
  1718.9 49.7 %copy-start.9 = (f32[32,4608]{1,0:T(8,128)S(1)}, f32[32,4608]{1,0:T(8,128)}, u32[]{:S(2)}) copy-start(f32[32,4608]{1,0:T(8,128)} %param.42) | copy-start | bytes 1769476
  1719.0 49.7 %copy-start.10 = (f32[32,4608]{1,0:T(8,128)S(1)}, f32[32,4608]{1,0:T(8,128)}, u32[]{:S(2)}) copy-start(f32[32,4608]{1,0:T(8,128)} %param.39) | copy-start | bytes 1769476
  1719.0 49.7 %copy-start.11 = (f32[32,4608]{1,0:T(8,128)S(1)}, f32[32,4608]{1,0:T(8,128)}, u32[]{:S(2)}) copy-start(f32[32,4608]{1,0:T(8,128)} %reduce-scatter.16.cloned.1.call-done) | copy-start | bytes 1769476
  1719.0 49.7 %copy-start.12 = (f32[32,4608]{1,0:T(8,128)S(1)}, f32[32,4608]{1,0:T(8,128)}, u32[]{:S(2)}) copy-start(f32[32,4608]{1,0:T(8,128)} %reduce-scatter.18.cloned.1.call-done) | copy-start | bytes 1769476
  (34 other events, 378.0 us)
Sparse Core Ops, SparseCore 0:
  11.5 72.2 all-gather.7
  87.4 54.9 all-gather.9
  145.8 80.6 all-gather.13
  229.7 80.6 all-gather.15
  313.6 80.6 all-gather.11
  498.4 132.6 reduce-scatter.21
  634.0 130.3 reduce-scatter.23
  766.6 143.9 reduce-scatter.13
  916.6 154.6 reduce-scatter.11
  1078.7 205.8 reduce-scatter.15
  1292.2 205.6 reduce-scatter.17
  1505.3 205.6 reduce-scatter.19
where the time goes:
time: 1790 us; the launch traced here: 1780 us
  waiting for transfers between devices  1290 us (72%)
  matrix products  214 us (12%)
  blocking collectives  172 us (10%)
  other arithmetic  62.2 us (3%)
  between operations  21.5 us (1%)
    reduce_scatter x1, waiting for transfers between devices, local(): lax.psum_scatter(up_weight_gradient, ('dp', 'seq'), scatter_dimension=0,...  211 us
    reduce_scatter x1, waiting for transfers between devices, local(): lax.psum_scatter(down_weight_gradient, ('dp', 'seq'), scatter_dimension=0...  211 us
    reduce_scatter x1, waiting for transfers between devices, local(): lax.psum_scatter(gate_weight_gradient, ('dp', 'seq'), scatter_dimension=0...  210 us
    unnamed x14, waiting for transfers between devices  174 us
    reduce_scatter x1, waiting for transfers between devices, local(): lax.psum_scatter(input_weight_gradient, ('dp', 'seq'), scatter_dimension=...  159 us
    reduce_scatter x1, waiting for transfers between devices, local(): lax.psum_scatter(output_weight_gradient, ('dp', 'seq'), scatter_dimension...  144 us
    all_gather x1, blocking collectives, local(): lax.all_gather(low_gains, ('dp', 'seq'), axis=1, tiled=True)  69.6 us
    all_gather x1, waiting for transfers between devices, local(): lax.all_gather(low_down, ('dp', 'seq'), axis=0, tiled=True)  67.9 us
  transfers between devices with their start and end apart: 14, of which 12 were waited for; matrix products, arithmetic and copies ran while one was open for 9% of the time, Pallas kernels for 0%

commit v1 on v0

--- a/solution.py
+++ b/solution.py
@@ -23,6 +23,100 @@
     devices = lax.axis_size(axis)
     pairs = [(i, i + by) for i in range(devices) if 0 <= i + by < devices]
     return lax.ppermute(shard, axis, pairs)
+
+
+def bits_of(size):
+    return size.bit_length() - 1
+
+
+def swap_bit(shard, bit):
+    devices = lax.axis_size("dp")
+    return lax.ppermute(shard, "dp", [(i, i ^ (1 << bit)) for i in range(devices)])
+
+
+def swap_seq(shard, by):
+    devices = lax.axis_size("seq")
+    return lax.ppermute(shard, "seq", [(i, (i + by) % devices) for i in range(devices)])
+
+
+def bit_order(flipped):
+    order = list(range(1, bits_of(lax.axis_size("dp"))))
+    return order[::-1] if flipped else order
+
+
+def collect(shard, flipped):
+    span = lax.axis_size("seq")
+    place = lax.axis_index("seq")
+    row = lax.axis_index("dp")
+    arrived = jnp.stack([shard] + [swap_seq(shard, by) for by in range(1, span)])
+    held = jnp.stack(
+        [
+            lax.dynamic_index_in_dim(arrived, (place - i + span) % span, 0, keepdims=False)
+            for i in range(span)
+        ]
+    )
+    seen = []
+    for bit in bit_order(flipped) + [0]:
+        other = swap_bit(held, bit)
+        upper = ((row >> bit) & 1) == 1
+        axis = sum(1 for b in seen if b > bit)
+        held = jnp.stack(
+            [jnp.where(upper, other, held), jnp.where(upper, held, other)], axis=axis
+        )
+        seen.append(bit)
+    return held
+
+
+def gather_rows(shard, flipped):
+    full = collect(shard.astype(jnp.bfloat16), flipped)
+    return full.reshape((-1, full.shape[-1]))
+
+
+def scatter_sum(parts, flipped):
+    span = lax.axis_size("seq")
+    place = lax.axis_index("seq")
+    row = lax.axis_index("dp")
+    kind = parts.dtype
+    left = list(range(bits_of(lax.axis_size("dp"))))
+    for bit in [0] + bit_order(flipped)[::-1]:
+        axis = sum(1 for b in left if b > bit)
+        mine = (row >> bit) & 1
+        away = lax.dynamic_index_in_dim(parts, 1 - mine, axis, keepdims=False)
+        kept = lax.dynamic_index_in_dim(parts, mine, axis, keepdims=False)
+        came = swap_bit(away, bit)
+        parts = (kept.astype(jnp.float32) + came.astype(jnp.float32)).astype(kind)
+        left.remove(bit)
+    total = lax.dynamic_index_in_dim(parts, place, 0, keepdims=False).astype(jnp.float32)
+    for by in range(1, span):
+        away = lax.dynamic_index_in_dim(parts, (place + by) % span, 0, keepdims=False)
+        total = total + swap_seq(away, by).astype(jnp.float32)
+    return total
+
+
+def scatter_rows(gradient, flipped):
+    span = lax.axis_size("seq")
+    bits = bits_of(lax.axis_size("dp"))
+    rows = gradient.shape[0] // ((1 << bits) * span)
+    parts = gradient.astype(jnp.bfloat16).reshape((2,) * bits + (span, rows, gradient.shape[1]))
+    return scatter_sum(parts, flipped)
+
+
+def sum_everywhere(value):
+    tile = jnp.full((8, 128), value, jnp.float32)
+    for axis in ("seq", "dp"):
+        devices = lax.axis_size(axis)
+        step = 1
+        while step < devices:
+            radix = 4 if step * 4 <= devices else 2
+            terms = [tile] + [
+                lax.ppermute(tile, axis, [(i, i ^ (k * step)) for i in range(devices)])
+                for k in range(1, radix)
+            ]
+            while len(terms) > 1:
+                terms = [terms[i] + terms[i + 1] for i in range(0, len(terms), 2)]
+            tile = terms[0]
+            step *= radix
+    return tile[0, 0]
 
 
 def adam_update(master, first, second, gradient, factor, rate):
@@ -61,31 +155,16 @@
     w_down_first,
     w_down_second,
 ):
-    low_gains = norm_gains.astype(jnp.bfloat16)
-    low_kernel = kernel.astype(jnp.bfloat16)
-    low_in = w_in.astype(jnp.bfloat16)
-    low_out = w_out.astype(jnp.bfloat16)
-    low_gate = w_gate.astype(jnp.bfloat16)
-    low_up = w_up.astype(jnp.bfloat16)
-    low_down = w_down.astype(jnp.bfloat16)
-    gathered = (
-        lax.all_gather(low_gains, ("dp", "seq"), axis=1, tiled=True),
-        lax.all_gather(low_kernel, ("dp", "seq"), axis=1, tiled=True),
-        lax.all_gather(low_in, ("dp", "seq"), axis=0, tiled=True),
-        lax.all_gather(low_out, ("dp", "seq"), axis=0, tiled=True),
-        lax.all_gather(low_gate, ("dp", "seq"), axis=0, tiled=True),
-        lax.all_gather(low_up, ("dp", "seq"), axis=0, tiled=True),
-        lax.all_gather(low_down, ("dp", "seq"), axis=0, tiled=True),
-    )
-    (
-        full_gains,
-        full_kernel,
-        collected_entry_matrix,
-        gathered_output_weight,
-        gathered_gate_weight,
-        gathered_up_weight,
-        gathered_down_weight,
-    ) = gathered
+    low_small = jnp.concatenate([norm_gains, kernel], axis=0).astype(jnp.bfloat16)
+    small = collect(low_small, False)
+    small = small.reshape((-1,) + low_small.shape).transpose(1, 0, 2).reshape(low_small.shape[0], -1)
+    full_gains = small[:2]
+    full_kernel = small[2:]
+    collected_entry_matrix = gather_rows(w_in, False)
+    gathered_output_weight = gather_rows(w_out, True)
+    gathered_gate_weight = gather_rows(w_gate, False)
+    gathered_up_weight = gather_rows(w_up, True)
+    gathered_down_weight = gather_rows(w_down, True)
     gain_wide = full_gains.astype(jnp.float32)
     taps = full_kernel.astype(jnp.float32)
     width = inputs.shape[2]
@@ -213,20 +292,29 @@
         + scale_one * zeta_one
         - values * scale_one**3 * jnp.mean(zeta_one * values, axis=-1, keepdims=True)
     )
-    gains_grad = jnp.stack([first_scale_derivative, gain_two_grad])
+    small_grads = jnp.concatenate(
+        [first_scale_derivative[None], gain_two_grad[None], kernel_grad], axis=0
+    )
+    columns = norm_gains.shape[1]
+    parts = small_grads.reshape(small_grads.shape[0], -1, columns).transpose(1, 0, 2)
+    parts = parts.reshape(
+        (2,) * bits_of(lax.axis_size("dp"))
+        + (lax.axis_size("seq"), small_grads.shape[0], columns)
+    )
+    small_shard = scatter_sum(parts, False)
     shards = (
-        lax.psum_scatter(gains_grad, ("dp", "seq"), scatter_dimension=1, tiled=True),
-        lax.psum_scatter(kernel_grad, ("dp", "seq"), scatter_dimension=1, tiled=True),
-        lax.psum_scatter(input_weight_gradient, ("dp", "seq"), scatter_dimension=0, tiled=True),
-        lax.psum_scatter(output_weight_gradient, ("dp", "seq"), scatter_dimension=0, tiled=True),
-        lax.psum_scatter(gate_weight_gradient, ("dp", "seq"), scatter_dimension=0, tiled=True),
-        lax.psum_scatter(up_weight_gradient, ("dp", "seq"), scatter_dimension=0, tiled=True),
-        lax.psum_scatter(down_weight_gradient, ("dp", "seq"), scatter_dimension=0, tiled=True),
+        small_shard[:2],
+        small_shard[2:],
+        scatter_rows(input_weight_gradient, False),
+        scatter_rows(output_weight_gradient, True),
+        scatter_rows(gate_weight_gradient, False),
+        scatter_rows(up_weight_gradient, True),
+        scatter_rows(down_weight_gradient, True),
     )
     squares = jnp.float32(0.0)
     for portion in shards:
         squares = squares + jnp.sum(portion * portion)
-    grad_norm = jnp.sqrt(lax.psum(squares, ("dp", "seq")))
+    grad_norm = jnp.sqrt(sum_everywhere(squares))
     factor = CLIP / jnp.maximum(grad_norm, CLIP)
     matrix_rate = RATE / math.sqrt(D)
     gains_first_new, gains_second_new, gains_new = adam_update(

time: 1790 us -> 992 us (0.55)
  waiting for transfers between devices: 1290 us -> 383 us
  blocking collectives: 172 us -> 0 us
  starting transfers between devices: 7.23 us -> 162 us
  other arithmetic: 62.2 us -> 170 us
  local copies, waits for them, and re-layouts: 9.9 us -> 72.9 us
  matrix products: 214 us -> 191 us
    reduce_scatter x5 -> x0, waiting for transfers between devices: 934 us -> none  [the longest x1 211 us: local(): lax.psum_scatter(up_weight_gradient, ('dp', 'seq'), scatter_dimension=0,...]
    ppermute x0 -> x79, waiting for transfers between devices: none -> 381 us  [the longest x36 307 us: swap_bit(): lax.ppermute(shard, 'dp', [(i, i ^ 1 << bit) for i in range(devices)])]
    all_gather x5 -> x0, waiting for transfers between devices: 181 us -> none  [the longest x1 67.9 us: local(): lax.all_gather(low_down, ('dp', 'seq'), axis=0, tiled=True)]
    unnamed x14 -> x0, waiting for transfers between devices: 174 us -> none
    ppermute x0 -> x79, starting transfers between devices: none -> 140 us  [the longest x36 99.1 us: swap_seq(): lax.ppermute(shard, 'seq', [(i, (i + by) % devices) for i in range(device...]
    all_gather x2 -> x0, blocking collectives: 133 us -> none  [the longest x1 69.6 us: local(): lax.all_gather(low_gains, ('dp', 'seq'), axis=1, tiled=True)]
    another operation x4 -> x57, other arithmetic: 8.57 us -> 87.3 us  [the longest x36 67.9 us: collect(): jnp.stack([jnp.where(upper, other, held), jnp.where(upper, held, other)],...]
    psum x1 -> x0, blocking collectives: 39.1 us -> none  [local(): grad_norm = jnp.sqrt(lax.psum(squares, ('dp', 'seq')))]
  transfers between devices with their start and end apart: 14 -> 81, of which waited for: 12 -> 35; matrix products, arithmetic and copies ran while one was open for 9% -> 25% of each run, Pallas kernels for 0% -> 0%
where the time goes in v1:
time: 992 us; the launch traced here: 987 us
  waiting for transfers between devices  383 us (39%)
  matrix products  191 us (19%)
  other arithmetic  170 us (17%)
  starting transfers between devices  162 us (16%)
  local copies, waits for them, and re-layouts  72.9 us (7%)
    ppermute x36, waiting for transfers between devices, swap_bit(): lax.ppermute(shard, 'dp', [(i, i ^ 1 << bit) for i in range(devices)])  307 us
    ppermute x36, starting transfers between devices, swap_seq(): lax.ppermute(shard, 'seq', [(i, (i + by) % devices) for i in range(device...  99.1 us
    ppermute x36, waiting for transfers between devices, swap_seq(): lax.ppermute(shard, 'seq', [(i, (i + by) % devices) for i in range(device...  71.1 us
    another operation x36, other arithmetic, collect(): jnp.stack([jnp.where(upper, other, held), jnp.where(upper, held, other)],...  67.9 us
    convert_element_type x15, other arithmetic, scatter_sum(): parts = (kept.astype(jnp.float32) + came.astype(jnp.float32)).astype(kind)  31.2 us
    ppermute x36, starting transfers between devices, swap_bit(): lax.ppermute(shard, 'dp', [(i, i ^ 1 << bit) for i in range(devices)])  30.7 us
    another operation x6, local copies, waits for them, and re-layouts, collect(): jnp.stack([jnp.where(upper, other, held), jnp.where(upper, held, other)],...  30.4 us
    dot_general x1, matrix products, local(): jnp.einsum('wyz,zm->wym', second_normed_input, gathered_up_weight, prefer...  29.1 us
  transfers between devices with their start and end apart: 81, of which 35 were waited for; matrix products, arithmetic and copies ran while one was open for 25% of the time, Pallas kernels for 0%

profile of v1, /device:TPU:0, one launch (start us, length us, event | category | flops | bytes accessed | tf_op | source)
XLA Modules:
  0.0 987.1 jit_solution(2703088521978031571)
XLA Ops:
  102.6 13.2 %collective-permute-done.32 = bf16[144,1024]{1,0:T(8,128)(2,1)S(1)} collective-permute-done((bf16[144,1024]{1,0:T(8,128)(2,1)S(1)}, bf16[144,1024]{1,0:T(8,128)(2,1)S(1)}, u32[]{:S(2)}, u32[]{:S(2)}) %collective-permute-start.32) | collective-permute-done | bytes 294944 | tf_op jit(solution)/shard_map/ppermute | solution.py:39
  131.1 18.6 %collective-permute-done.22 = bf16[4,32,4608]{2,1,0:T(8,128)(2,1)S(1)} collective-permute-done((bf16[4,32,4608]{2,1,0:T(8,128)(2,1)S(1)}, bf16[4,32,4608]{2,1,0:T(8,128)(2,1)S(1)}, u32[]{:S(2)}, u32[]{:S(2)}) %collective-permute-start.22) | collective-permute-done | bytes 1179680 | tf_op jit(solution)/shard_map/ppermute | solution.py:34
  158.2 30.8 %collective-permute-done.10 = bf16[2,4,32,3072]{3,2,1,0:T(8,128)(2,1)S(1)} collective-permute-done((bf16[2,4,32,3072]{3,2,1,0:T(8,128)(2,1)S(1)}, bf16[2,4,32,3072]{3,2,1,0:T(8,128)(2,1)S(1)}, u32[]{:S(2)}, u32[]{:S(2)}) %collective-permute-start.10) | collective-permute-done | bytes 1572896 | tf_op jit(solution)/shard_map/ppermute | solution.py:34
  189.6 10.6 %collective-permute-done.29 = bf16[2,4,32,4608]{3,2,1,0:T(8,128)(2,1)S(1)} collective-permute-done((bf16[2,4,32,4608]{3,2,1,0:T(8,128)(2,1)S(1)}, bf16[2,4,32,4608]{3,2,1,0:T(8,128)(2,1)S(1)}, u32[]{:S(2)}, u32[]{:S(2)}) %collective-permute-start.29) | collective-permute-done | bytes 2359328 | tf_op jit(solution)/shard_map/ppermute | solution.py:34
  203.0 34.3 %collective-permute-done.23 = bf16[2,4,32,4608]{3,2,1,0:T(8,128)(2,1)} collective-permute-done((bf16[2,4,32,4608]{3,2,1,0:T(8,128)(2,1)S(1)}, bf16[2,4,32,4608]{3,2,1,0:T(8,128)(2,1)}, u32[]{:S(2)}, u32[]{:S(2)}) %collective-permute-start.23) | collective-permute-done | bytes 2359328 | tf_op jit(solution)/shard_map/ppermute | solution.py:34
  274.0 20.0 %collective-permute-start.12 = (bf16[4,2,1024]{2,1,0:T(2,128)(2,1)S(1)}, bf16[4,2,1024]{2,1,0:T(2,128)(2,1)S(1)}, u32[]{:S(2)}, u32[]{:S(2)}) collective-permute-start(bf16[4,2,1024]{2,1,0:T(2,128)(2,1)S(1)} %slice.121), channel_id=1, source_target_pairs={{0,1},{1,2},{2,3},{4,5},{5,6},{6,7},{8,9},{9,10},{10,11},{12,13},{... | collective-permute-start | bytes 49160 | tf_op jit(solution)/shard_map/ppermute | solution.py:25
  382.0 16.6 %fusion.89 = f32[4,256,4608]{2,1,0:T(8,128)} fusion(bf16[4,256,1024]{2,1,0:T(8,128)(2,1)S(1)} %copy-done.35, bf16[1024,4608,1]{1,0,2:T(8,128)(2,1)} %bitcast.361), kind=kOutput, calls=%fused_computation.327 | convolution fusion | flops 9663676416 | bytes 30408704 | tf_op jit(solution)/shard_map/wyz,zm->wym/dot_general | solution.py:202
  398.6 13.1 %fusion.90 = f32[4608,4,256]{0,2,1:T(8,128)} fusion(bf16[4608,1024,1]{1,0,2:T(8,128)(2,1)S(1)} %bitcast.357, bf16[4,256,1024]{2,1,0:T(8,128)(2,1)S(1)} %copy-done.39), kind=kOutput, calls=%fused_computation.328 | convolution fusion | flops 9663676416 | bytes 30408704 | tf_op jit(solution)/shard_map/uar,tr->uat/dot_general | solution.py:220
  411.7 29.1 %fusion.2 = (bf16[4,256,4608]{2,1,0:T(8,128)(2,1)}, bf16[4,256,4608]{2,1,0:T(8,128)(2,1)}, bf16[4,256,4608]{2,1,0:T(8,128)(2,1)}) fusion(f32[4608,4,256]{0,2,1:T(8,128)} %fusion.90, f32[4,256,4608]{2,1,0:T(8,128)} %fusion.89, bf16[4,256,1024]{2,1,0:T(8,128)(2,1)S(1)} %copy-done.35, bf16[1024,4608,1]{1,0,2:T(8,128)(2,1)} %bitcast.358), kind=kOutput, calls=%fused_computation.7 | convolution fusion | flops 9734455296 | bytes 77594624 | tf_op jit(solution)/shard_map/wyz,zm->wym/dot_general | solution.py:205
  440.8 16.1 %bitcast_convert_fusion.1 = bf16[1024,4608]{1,0:T(8,128)(2,1)} fusion(bf16[4,256,1024]{2,1,0:T(8,128)(2,1)S(1)} %copy-done.35, bf16[4,256,4608]{2,1,0:T(8,128)(2,1)} %get-tuple-element.67), kind=kOutput, calls=%fused_computation.1 | convolution fusion | flops 9668395008 | bytes 20971520 | tf_op jit(solution)/shard_map/rbz,rbx->zx/dot_general | solution.py:239
  456.9 14.0 %fusion.91 = f32[4,256,1024]{2,1,0:T(8,128)} fusion(bf16[4,256,4608]{2,1,0:T(8,128)(2,1)S(1)} %copy-done.83, bf16[1024,4608,1]{1,0,2:T(8,128)(2,1)} %bitcast.359), kind=kOutput, calls=%fused_computation.329 | convolution fusion | flops 9663676416 | bytes 23068672 | tf_op jit(solution)/shard_map/npg,kg->npk/dot_general | solution.py:233
  470.9 16.6 %multiply_reduce_fusion.3 = (f32[1024]{0:T(1024)S(1)}, f32[4,256]{1,0:T(4,128)S(1)}, f32[4,256,1024]{2,1,0:T(8,128)S(1)}) fusion(f32[4,256,1024]{2,1,0:T(8,128)S(1)} %copy-done.10, f32[4,256]{1,0:T(4,128)S(1)} %copy-done.61, f32[1024]{0:T(1024)S(1)} %copy-done.59, f32[4,256,1024]{2,1,0:T(8,128)} %fusion.91, bf16[4,256,4608]{2,1,0:T(8,128)(2,1)} %get-tuple-element.66, ...), kind=kOutput, calls=%fused_computation.72 | convolution fusion | flops 9671014400 | bytes 31473664 | tf_op jit(solution)/shard_map/npg,kg->npk/dot_general | solution.py:230
  497.4 12.3 %bitcast_convert_fusion = bf16[4608,1024]{1,0:T(8,128)(2,1)} fusion(bf16[4,256,4608]{2,1,0:T(8,128)(2,1)S(1)} %bitcast.399, bf16[4,256,1024]{2,1,0:T(8,128)(2,1)S(1)} %copy-done.40), kind=kOutput, calls=%fused_computation | convolution fusion | flops 9668395008 | bytes 20971520 | tf_op jit(solution)/shard_map/vna,vnw->aw/dot_general | solution.py:223
  557.6 11.6 %fusion.19 = (f32[1024]{0:T(1024)S(1)}, f32[4,256]{1,0:T(4,128)}, f32[4,256,1024]{2,1,0:T(8,128)}) fusion(bf16[4,256,1024]{2,1,0:T(8,128)(2,1)S(1)} %copy-done.19, f32[4,256]{1,0:T(4,128)S(1)} %copy-done.75, f32[1024]{0:T(1024)S(1)} %copy-done.77, bf16[1024,3072,1]{1,0,2:T(8,128)(2,1)S(1)} %bitcast.369, bf16[4,256,1024]{2,1,0:T(8,128)(2,1)} %multiply_convert_fusion.1, ...), kind=kOutput, calls=%fused_computation.59 | convolution fusion | flops 6468663296 | bytes 18890752 | tf_op jit(solution)/shard_map/fxh,dh->fxd/dot_general | solution.py:279
  569.6 9.9 %bitcast_convert_fusion.3 = bf16[1024,3072]{1,0:T(8,128)(2,1)S(1)} fusion(bf16[4,256,1024]{2,1,0:T(8,128)(2,1)} %multiply_convert_fusion.1, bf16[4,256,1024]{2,1,0:T(8,128)(2,1)} %get-tuple-element.89, bf16[4,256,1024]{2,1,0:T(8,128)(2,1)} %copy-done.33, bf16[4,256,1024]{2,1,0:T(8,128)(2,1)S(1)} %copy-done.19, f32[1024]{0:T(1024)S(1)} %copy-done.77, ...), kind=kOutput, calls=%fused_computation.12 | convolution fusion | flops 6468665344 | bytes 14688256 | tf_op jit(solution)/shard_map/ncr,ncj->rj/dot_general | solution.py:285
  587.3 12.8 %bitcast_convert_fusion.2 = bf16[1024,4608]{1,0:T(8,128)(2,1)S(1)} fusion(bf16[4,256,1024]{2,1,0:T(8,128)(2,1)S(1)} %copy-done.36, bf16[4,256,4608]{2,1,0:T(8,128)(2,1)} %get-tuple-element.66), kind=kOutput, calls=%fused_computation.2 | convolution fusion | flops 9668395008 | bytes 20971520 | tf_op jit(solution)/shard_map/rbz,rbx->zx/dot_general | solution.py:236
  645.6 20.1 %collective-permute-done.45 = bf16[2,4,32,3072]{3,2,1,0:T(8,128)(2,1)} collective-permute-done((bf16[2,4,32,3072]{3,2,1,0:T(8,128)(2,1)}, bf16[2,4,32,3072]{3,2,1,0:T(8,128)(2,1)}, u32[]{:S(2)}, u32[]{:S(2)}) %collective-permute-start.45) | collective-permute-done | bytes 1572896 | tf_op jit(solution)/shard_map/ppermute | solution.py:34
  674.8 82.7 %collective-permute-done.46 = bf16[4,32,3072]{2,1,0:T(8,128)(2,1)S(1)} collective-permute-done((bf16[4,32,3072]{2,1,0:T(8,128)(2,1)S(1)}, bf16[4,32,3072]{2,1,0:T(8,128)(2,1)S(1)}, u32[]{:S(2)}, u32[]{:S(2)}) %collective-permute-start.46) | collective-permute-done | bytes 786464 | tf_op jit(solution)/shard_map/ppermute | solution.py:34
  784.1 37.8 %collective-permute-done.57 = bf16[2,4,32,4608]{3,2,1,0:T(8,128)(2,1)} collective-permute-done((bf16[2,4,32,4608]{3,2,1,0:T(8,128)(2,1)}, bf16[2,4,32,4608]{3,2,1,0:T(8,128)(2,1)}, u32[]{:S(2)}, u32[]{:S(2)}) %collective-permute-start.57) | collective-permute-done | bytes 2359328 | tf_op jit(solution)/shard_map/ppermute | solution.py:34
  825.8 40.1 %collective-permute-done.64 = bf16[4,32,4608]{2,1,0:T(8,128)(2,1)S(1)} collective-permute-done((bf16[4,32,4608]{2,1,0:T(8,128)(2,1)S(1)}, bf16[4,32,4608]{2,1,0:T(8,128)(2,1)S(1)}, u32[]{:S(2)}, u32[]{:S(2)}) %collective-permute-start.64) | collective-permute-done | bytes 1179680 | tf_op jit(solution)/shard_map/ppermute | solution.py:34
  880.7 10.9 %collective-permute-done.59 = bf16[32,4608]{1,0:T(8,128)(2,1)S(1)} collective-permute-done((bf16[32,4608]{1,0:T(8,128)(2,1)S(1)}, bf16[32,4608]{1,0:T(8,128)(2,1)S(1)}, u32[]{:S(2)}, u32[]{:S(2)}) %collective-permute-start.59) | collective-permute-done | bytes 294944 | tf_op jit(solution)/shard_map/ppermute | solution.py:39
  891.6 24.6 %collective-permute-start.71 = (bf16[144,1024]{1,0:T(8,128)(2,1)}, bf16[144,1024]{1,0:T(8,128)(2,1)}, u32[]{:S(2)}, u32[]{:S(2)}) collective-permute-start(bf16[144,1024]{1,0:T(8,128)(2,1)} %get-tuple-element.105), channel_id=1, source_target_pairs={{0,1},{1,2},{2,3},{3,0},{4,5},{5,6},{6,7},{7,4},{8,9},{9,10},{10,1... | collective-permute-start | bytes 884744 | tf_op jit(solution)/shard_map/ppermute | solution.py:39
  918.0 13.5 %collective-permute-start.73 = (bf16[144,1024]{1,0:T(8,128)(2,1)}, bf16[144,1024]{1,0:T(8,128)(2,1)}, u32[]{:S(2)}, u32[]{:S(2)}) collective-permute-start(bf16[144,1024]{1,0:T(8,128)(2,1)} %get-tuple-element.106), channel_id=1, source_target_pairs={{0,3},{1,0},{2,1},{3,2},{4,7},{5,4},{6,5},{7,6},{8,11},{9,8},{10,9... | collective-permute-start | bytes 884744 | tf_op jit(solution)/shard_map/ppermute | solution.py:39
  948.0 16.7 %add_convert_fusion = bf16[4,256,1024]{2,1,0:T(8,128)(2,1)} fusion(f32[4,256,1024]{2,1,0:T(8,128)} %copy-done.9, bf16[4,256,4608]{2,1,0:T(8,128)(2,1)} %get-tuple-element.68, bf16[4608,1024,1]{1,0,2:T(8,128)(2,1)} %bitcast.356), kind=kOutput, calls=%fused_computation.79 | convolution fusion | flops 9665773568 | bytes 25165824 | tf_op jit(solution)/shard_map/vyk,kx->vyx/dot_general | solution.py:213
  (533 shorter events, 451.4 us)
Async XLA Ops:
  2.7 68.7 %collective-permute-start.19 = (bf16[32,4608]{1,0:T(8,128)(2,1)}, bf16[32,4608]{1,0:T(8,128)(2,1)}, u32[]{:S(2)}, u32[]{:S(2)}) collective-permute-start(bf16[32,4608]{1,0:T(8,128)(2,1)} %convert_element_type.368), channel_id=1, source_target_pairs={{0,1},{1,2},{2,3},{3,0},{4,5},{5,6},{6,7},{7,4},{8,9},{9,10},{10,1... | collective-permute-start | bytes 884744 | tf_op jit(solution)/shard_map/ppermute | solution.py:39
  5.7 65.8 %collective-permute-start.20 = (bf16[32,4608]{1,0:T(8,128)(2,1)}, bf16[32,4608]{1,0:T(8,128)(2,1)}, u32[]{:S(2)}, u32[]{:S(2)}) collective-permute-start(bf16[32,4608]{1,0:T(8,128)(2,1)} %convert_element_type.368), channel_id=1, source_target_pairs={{0,2},{1,3},{2,0},{3,1},{4,6},{5,7},{6,4},{7,5},{8,10},{9,11},{10,... | collective-permute-start | bytes 884744 | tf_op jit(solution)/shard_map/ppermute | solution.py:39
  125.0 64.0 %collective-permute-start.10 = (bf16[2,4,32,3072]{3,2,1,0:T(8,128)(2,1)S(1)}, bf16[2,4,32,3072]{3,2,1,0:T(8,128)(2,1)S(1)}, u32[]{:S(2)}, u32[]{:S(2)}) collective-permute-start(bf16[2,4,32,3072]{3,2,1,0:T(8,128)(2,1)S(1)} %pad_maximum_fusion.15), channel_id=1, source_target_pairs={{0,16},{4,20},{8,24},{12,28},{16,0},{20,4},{24,8},{28,12},{1,17},{... | collective-permute-start | bytes 4718600 | tf_op jit(solution)/shard_map/ppermute | solution.py:34
  130.5 69.8 %collective-permute-start.29 = (bf16[2,4,32,4608]{3,2,1,0:T(8,128)(2,1)S(1)}, bf16[2,4,32,4608]{3,2,1,0:T(8,128)(2,1)S(1)}, u32[]{:S(2)}, u32[]{:S(2)}) collective-permute-start(bf16[2,4,32,4608]{3,2,1,0:T(8,128)(2,1)S(1)} %pad_maximum_fusion.12), channel_id=1, source_target_pairs={{0,8},{4,12},{8,0},{12,4},{16,24},{20,28},{24,16},{28,20},{1,9},{5... | collective-permute-start | bytes 7077896 | tf_op jit(solution)/shard_map/ppermute | solution.py:34
  150.1 87.2 %collective-permute-start.23 = (bf16[2,4,32,4608]{3,2,1,0:T(8,128)(2,1)S(1)}, bf16[2,4,32,4608]{3,2,1,0:T(8,128)(2,1)}, u32[]{:S(2)}, u32[]{:S(2)}) collective-permute-start(bf16[2,4,32,4608]{3,2,1,0:T(8,128)(2,1)S(1)} %pad_maximum_fusion.11), channel_id=1, source_target_pairs={{0,16},{4,20},{8,24},{12,28},{16,0},{20,4},{24,8},{28,12},{1,17},{... | collective-permute-start | bytes 7077896 | tf_op jit(solution)/shard_map/ppermute | solution.py:34
  155.7 93.7 %collective-permute-start.35 = (bf16[2,4,144,1024]{3,2,1,0:T(8,128)(2,1)S(1)}, bf16[2,4,144,1024]{3,2,1,0:T(8,128)(2,1)}, u32[]{:S(2)}, u32[]{:S(2)}) collective-permute-start(bf16[2,4,144,1024]{3,2,1,0:T(8,128)(2,1)S(1)} %pad_maximum_fusion.13), channel_id=1, source_target_pairs={{0,8},{4,12},{8,0},{12,4},{16,24},{20,28},{24,16},{28,20},{1,9},{5... | collective-permute-start | bytes 7077896 | tf_op jit(solution)/shard_map/ppermute | solution.py:34
  189.5 63.3 %collective-permute-start.11 = (bf16[2,2,4,32,3072]{4,3,2,1,0:T(8,128)(2,1)S(1)}, bf16[2,2,4,32,3072]{4,3,2,1,0:T(8,128)(2,1)S(1)}, u32[]{:S(2)}, u32[]{:S(2)}) collective-permute-start(bf16[2,2,4,32,3072]{4,3,2,1,0:T(8,128)(2,1)S(1)} %pad_maximum_fusion.8), channel_id=1, source_target_pairs={{0,4},{4,0},{8,12},{12,8},{16,20},{20,16},{24,28},{28,24},{1,5},{5... | collective-permute-start | bytes 9437192 | tf_op jit(solution)/shard_map/ppermute | solution.py:34
  203.0 107.9 %collective-permute-start.30 = (bf16[2,2,4,32,4608]{4,3,2,0,1:T(8,128)(2,1)}, bf16[2,2,4,32,4608]{4,3,2,0,1:T(8,128)(2,1)}, u32[]{:S(2)}, u32[]{:S(2)}) collective-permute-start(bf16[2,2,4,32,4608]{4,3,2,0,1:T(8,128)(2,1)} %pad_maximum_fusion.6), channel_id=1, source_target_pairs={{0,4},{4,0},{8,12},{12,8},{16,20},{20,16},{24,28},{28,24},{1,5},{5... | collective-permute-start | bytes 14155784 | tf_op jit(solution)/shard_map/ppermute | solution.py:34
  242.2 91.4 %collective-permute-start.24 = (bf16[2,2,4,32,4608]{4,3,2,0,1:T(8,128)(2,1)}, bf16[2,2,4,32,4608]{4,3,2,0,1:T(8,128)(2,1)}, u32[]{:S(2)}, u32[]{:S(2)}) collective-permute-start(bf16[2,2,4,32,4608]{4,3,2,0,1:T(8,128)(2,1)} %pad_maximum_fusion.5), channel_id=1, source_target_pairs={{0,4},{4,0},{8,12},{12,8},{16,20},{20,16},{24,28},{28,24},{1,5},{5... | collective-permute-start | bytes 14155784 | tf_op jit(solution)/shard_map/ppermute | solution.py:34
  296.6 60.9 %collective-permute-start.36 = (bf16[2,2,4,144,1024]{4,3,2,0,1:T(8,128)(2,1)}, bf16[2,2,4,144,1024]{4,3,2,0,1:T(8,128)(2,1)}, u32[]{:S(2)}, u32[]{:S(2)}) collective-permute-start(bf16[2,2,4,144,1024]{4,3,2,0,1:T(8,128)(2,1)} %pad_maximum_fusion.7), channel_id=1, source_target_pairs={{0,4},{4,0},{8,12},{12,8},{16,20},{20,16},{24,28},{28,24},{1,5},{5... | collective-permute-start | bytes 14155784 | tf_op jit(solution)/shard_map/ppermute | solution.py:34
  519.7 111.7 %collective-permute-start.68 = (bf16[2,2,4,144,1024]{4,3,2,0,1:T(8,128)(2,1)}, bf16[2,2,4,144,1024]{4,3,2,0,1:T(8,128)(2,1)}, u32[]{:S(2)}, u32[]{:S(2)}) collective-permute-start(bf16[2,2,4,144,1024]{4,3,2,0,1:T(8,128)(2,1)} %bitcast.341), channel_id=1, source_target_pairs={{0,4},{4,0},{8,12},{12,8},{16,20},{20,16},{24,28},{28,24},{1,5},{5... | collective-permute-start | bytes 14155784 | tf_op jit(solution)/shard_map/ppermute | solution.py:34
  529.6 109.9 %collective-permute-start.62 = (bf16[2,2,4,32,4608]{4,3,2,0,1:T(8,128)(2,1)}, bf16[2,2,4,32,4608]{4,3,2,0,1:T(8,128)(2,1)}, u32[]{:S(2)}, u32[]{:S(2)}) collective-permute-start(bf16[2,2,4,32,4608]{4,3,2,0,1:T(8,128)(2,1)} %bitcast.342), channel_id=1, source_target_pairs={{0,4},{4,0},{8,12},{12,8},{16,20},{20,16},{24,28},{28,24},{1,5},{5... | collective-permute-start | bytes 14155784 | tf_op jit(solution)/shard_map/ppermute | solution.py:34
  622.0 47.6 %collective-permute-start.56 = (bf16[2,2,4,32,4608]{4,3,2,1,0:T(8,128)(2,1)}, bf16[2,2,4,32,4608]{4,3,2,1,0:T(8,128)(2,1)}, u32[]{:S(2)}, u32[]{:S(2)}) collective-permute-start(bf16[2,2,4,32,4608]{4,3,2,1,0:T(8,128)(2,1)} %dynamic-slice_bitcast_fusion), channel_id=1, source_target_pairs={{0,4},{4,0},{8,12},{12,8},{16,20},{20,16},{24,28},{28,24},{1,5},{5... | collective-permute-start | bytes 14155784 | tf_op jit(solution)/shard_map/ppermute | solution.py:34
  638.1 137.4 %collective-permute-start.69 = (bf16[2,4,144,1024]{3,2,1,0:T(8,128)(2,1)}, bf16[2,4,144,1024]{3,2,1,0:T(8,128)(2,1)}, u32[]{:S(2)}, u32[]{:S(2)}) collective-permute-start(bf16[2,4,144,1024]{3,2,1,0:T(8,128)(2,1)} %dynamic-slice_bitcast_fusion.2), channel_id=1, source_target_pairs={{0,8},{4,12},{8,0},{12,4},{16,24},{20,28},{24,16},{28,20},{1,9},{5... | collective-permute-start | bytes 7077896 | tf_op jit(solution)/shard_map/ppermute | solution.py:34
  645.1 135.4 %collective-permute-start.63 = (bf16[2,4,32,4608]{3,2,1,0:T(8,128)(2,1)}, bf16[2,4,32,4608]{3,2,1,0:T(8,128)(2,1)}, u32[]{:S(2)}, u32[]{:S(2)}) collective-permute-start(bf16[2,4,32,4608]{3,2,1,0:T(8,128)(2,1)} %dynamic-slice_bitcast_fusion.3), channel_id=1, source_target_pairs={{0,8},{4,12},{8,0},{12,4},{16,24},{20,28},{24,16},{28,20},{1,9},{5... | collective-permute-start | bytes 7077896 | tf_op jit(solution)/shard_map/ppermute | solution.py:34
  667.9 89.6 %collective-permute-start.46 = (bf16[4,32,3072]{2,1,0:T(8,128)(2,1)S(1)}, bf16[4,32,3072]{2,1,0:T(8,128)(2,1)S(1)}, u32[]{:S(2)}, u32[]{:S(2)}) collective-permute-start(bf16[4,32,3072]{2,1,0:T(8,128)(2,1)S(1)} %dynamic-slice_bitcast_fusion.9), channel_id=1, source_target_pairs={{0,8},{4,12},{8,0},{12,4},{16,24},{20,28},{24,16},{28,20},{1,9},{5... | collective-permute-start | bytes 2359304 | tf_op jit(solution)/shard_map/ppermute | solution.py:34
  767.5 54.5 %collective-permute-start.57 = (bf16[2,4,32,4608]{3,2,1,0:T(8,128)(2,1)}, bf16[2,4,32,4608]{3,2,1,0:T(8,128)(2,1)}, u32[]{:S(2)}, u32[]{:S(2)}) collective-permute-start(bf16[2,4,32,4608]{3,2,1,0:T(8,128)(2,1)} %dynamic-slice_bitcast_fusion.4), channel_id=1, source_target_pairs={{0,16},{4,20},{8,24},{12,28},{16,0},{20,4},{24,8},{28,12},{1,17},{... | collective-permute-start | bytes 7077896 | tf_op jit(solution)/shard_map/ppermute | solution.py:34
  779.4 92.9 %collective-permute-start.70 = (bf16[4,144,1024]{2,1,0:T(8,128)(2,1)S(1)}, bf16[4,144,1024]{2,1,0:T(8,128)(2,1)S(1)}, u32[]{:S(2)}, u32[]{:S(2)}) collective-permute-start(bf16[4,144,1024]{2,1,0:T(8,128)(2,1)S(1)} %dynamic-slice_bitcast_fusion.6), channel_id=1, source_target_pairs={{0,16},{4,20},{8,24},{12,28},{16,0},{20,4},{24,8},{28,12},{1,17},{... | collective-permute-start | bytes 3538952 | tf_op jit(solution)/shard_map/ppermute | solution.py:34
  783.0 82.9 %collective-permute-start.64 = (bf16[4,32,4608]{2,1,0:T(8,128)(2,1)S(1)}, bf16[4,32,4608]{2,1,0:T(8,128)(2,1)S(1)}, u32[]{:S(2)}, u32[]{:S(2)}) collective-permute-start(bf16[4,32,4608]{2,1,0:T(8,128)(2,1)S(1)} %dynamic-slice_bitcast_fusion.7), channel_id=1, source_target_pairs={{0,16},{4,20},{8,24},{12,28},{16,0},{20,4},{24,8},{28,12},{1,17},{... | collective-permute-start | bytes 3538952 | tf_op jit(solution)/shard_map/ppermute | solution.py:34
  824.3 45.0 %collective-permute-start.58 = (bf16[4,32,4608]{2,1,0:T(8,128)(2,1)S(1)}, bf16[4,32,4608]{2,1,0:T(8,128)(2,1)S(1)}, u32[]{:S(2)}, u32[]{:S(2)}) collective-permute-start(bf16[4,32,4608]{2,1,0:T(8,128)(2,1)S(1)} %dynamic-slice_bitcast_fusion.8), channel_id=1, source_target_pairs={{0,8},{4,12},{8,0},{12,4},{16,24},{20,28},{24,16},{28,20},{1,9},{5... | collective-permute-start | bytes 3538952 | tf_op jit(solution)/shard_map/ppermute | solution.py:34
  868.4 65.4 %collective-permute-start.66 = (bf16[32,4608]{1,0:T(8,128)(2,1)}, bf16[32,4608]{1,0:T(8,128)(2,1)}, u32[]{:S(2)}, u32[]{:S(2)}) collective-permute-start(bf16[32,4608]{1,0:T(8,128)(2,1)} %get-tuple-element.110), channel_id=1, source_target_pairs={{0,2},{1,3},{2,0},{3,1},{4,6},{5,7},{6,4},{7,5},{8,10},{9,11},{10,... | collective-permute-start | bytes 884744 | tf_op jit(solution)/shard_map/ppermute | solution.py:39
  872.3 45.8 %collective-permute-start.61 = (bf16[32,4608]{1,0:T(8,128)(2,1)S(1)}, bf16[32,4608]{1,0:T(8,128)(2,1)S(1)}, u32[]{:S(2)}, u32[]{:S(2)}) collective-permute-start(bf16[32,4608]{1,0:T(8,128)(2,1)S(1)} %get-tuple-element.112), channel_id=1, source_target_pairs={{0,3},{1,0},{2,1},{3,2},{4,7},{5,4},{6,5},{7,6},{8,11},{9,8},{10,9... | collective-permute-start | bytes 884744 | tf_op jit(solution)/shard_map/ppermute | solution.py:39
  878.9 54.9 %collective-permute-start.67 = (bf16[32,4608]{1,0:T(8,128)(2,1)}, bf16[32,4608]{1,0:T(8,128)(2,1)}, u32[]{:S(2)}, u32[]{:S(2)}) collective-permute-start(bf16[32,4608]{1,0:T(8,128)(2,1)} %get-tuple-element.109), channel_id=1, source_target_pairs={{0,3},{1,0},{2,1},{3,2},{4,7},{5,4},{6,5},{7,6},{8,11},{9,8},{10,9... | collective-permute-start | bytes 884744 | tf_op jit(solution)/shard_map/ppermute | solution.py:39
  891.6 45.7 %collective-permute-start.71 = (bf16[144,1024]{1,0:T(8,128)(2,1)}, bf16[144,1024]{1,0:T(8,128)(2,1)}, u32[]{:S(2)}, u32[]{:S(2)}) collective-permute-start(bf16[144,1024]{1,0:T(8,128)(2,1)} %get-tuple-element.105), channel_id=1, source_target_pairs={{0,1},{1,2},{2,3},{3,0},{4,5},{5,6},{6,7},{7,4},{8,9},{9,10},{10,1... | collective-permute-start | bytes 884744 | tf_op jit(solution)/shard_map/ppermute | solution.py:39
  (154 other events, 4228.0 us)
